TPU v7x, 32 devices: a whole 2x2x4 slice. The times are simulated.
32 devices in a mesh: blk: 4 (over y, x), head: 8 (over z, core).
Axes of the slice: x: 2, y: 2, z: 4, core: 2. Of those that a mesh axis runs over, the one named last changes fastest.
Arguments:
- queries: bfloat16 [4096, 4096], P(('blk', 'head')), may hold values from -14 to 14
- keys: bfloat16 [4096, 4096], P(('blk', 'head')), may hold values from -14 to 14
- values: bfloat16 [4096, 4096], P(('blk', 'head')), may hold values from -15 to 15
- key_blocks: int32 [8, 6], replicated, may hold values from 0 to 7, as said below
- counts: int32 [8], replicated, may hold values from 3 to 6, as said below
Outputs:
- attended: bfloat16 [4096, 4096], P(('blk', 'head'))
Inputs may be any that keep to these rules, and one draw needn't show every extreme that they name: `key_blocks`: row b lists, in slots below counts[b], distinct key blocks that lie in the cycle shard of b (shard = block // 2) or in one of the two shards beside it on the closed cycle of 4 shards; slots 0, 1, 2 hold b, b - 1 and b + 1 modulo 8; unused slots repeat slot 0. `counts`: some row uses all 6 slots and some row uses 3.
All inputs are finite; a program needn't handle non-finite values.
Results may differ from a plain program's by a relative error of at most 0.0036.
Values may be sent and summed in bfloat16 or wider, within the bound.
A program may use at most 64 MiB of HBM per device.

v0:
```python
import jax
import jax.numpy as jnp
from jax import lax
from jax.sharding import PartitionSpec as P

HD = 128
BLOCK = 512
MAXB = 6


def from_behind(value, axis, steps):
    count = lax.axis_size(axis)
    pairs = [(source, (source + steps) % count) for source in range(count)]
    return lax.ppermute(value, axis, pairs)


def attend_shard(query_rows, context, listed_rows, count_rows):
    scale = HD ** (-0.5)
    group_rows = query_rows.shape[0]
    heads_local = query_rows.shape[1] // HD
    blocks_here = group_rows // BLOCK
    q_blocks = query_rows.reshape(blocks_here, BLOCK, heads_local, HD)
    pair_blocks = context.reshape(2, 3 * blocks_here, BLOCK, heads_local, HD)
    slot_ids = jnp.arange(MAXB, dtype=jnp.int32)

    def attend_block(inputs):
        query_block, listed, amount = inputs
        chosen = pair_blocks[:, listed]
        usable = (slot_ids < amount)[None, None, :, None]
        scores = (
            jnp.einsum("qhd,jkhd->hqjk", query_block, chosen[0], preferred_element_type=jnp.float32)
            * scale
        )
        top = jnp.max(jnp.where(usable, scores, -jnp.inf), axis=(2, 3), keepdims=True)
        expo = jnp.where(usable, jnp.exp(scores - top), 0.0)
        total = jnp.sum(expo, axis=(2, 3))
        weights = expo.astype(jnp.bfloat16)
        mixed = jnp.einsum("hqjk,jkhd->qhd", weights, chosen[1], preferred_element_type=jnp.float32)
        mixed = mixed / jnp.transpose(total)[:, :, None]
        return mixed.astype(jnp.bfloat16).reshape(BLOCK, heads_local * HD)

    result = lax.map(attend_block, (q_blocks, listed_rows, count_rows))
    return result.reshape(group_rows, heads_local * HD)


def local(queries, keys, values, key_blocks, counts):
    cycle_size = lax.axis_size("blk")
    query_rows = lax.all_to_all(queries, "head", split_axis=1, concat_axis=0, tiled=True)
    head_pair = lax.all_to_all(
        jnp.stack([keys, values]), "head", split_axis=2, concat_axis=1, tiled=True
    )
    earlier = from_behind(head_pair, "blk", 1)
    later = from_behind(head_pair, "blk", -1)
    context = jnp.concatenate([earlier, head_pair, later], axis=1)
    blocks_here = query_rows.shape[0] // BLOCK
    total_blocks = blocks_here * cycle_size
    first_block = lax.axis_index("blk") * blocks_here
    listed_rows = lax.dynamic_slice_in_dim(key_blocks, first_block, blocks_here, 0)
    count_rows = lax.dynamic_slice_in_dim(counts, first_block, blocks_here, 0)
    local_index = jnp.mod(listed_rows - first_block + blocks_here, total_blocks)
    attended_rows = attend_shard(query_rows, context, local_index, count_rows)
    return lax.all_to_all(attended_rows, "head", split_axis=0, concat_axis=1, tiled=True)


def solution(mesh):
    placed = (
        P(("blk", "head"), None),
        P(("blk", "head"), None),
        P(("blk", "head"), None),
        P(),
        P(),
    )
    return jax.shard_map(
        local, mesh=mesh, in_specs=placed, out_specs=P(("blk", "head"), None), check_vma=False
    )
```

profile of v0, /device:TPU:1, one launch (start us, length us, event | category | flops | bytes accessed | tf_op | source)
XLA Modules:
  0.0 299.0 jit_solution(11622400577102586438)
XLA Ops:
  0.0 3.1 %pad_maximum_fusion.1 = bf16[2,128,4096]{2,1,0:T(8,128)(2,1)} fusion(bf16[1,128,4096]{2,1,0:T(8,128)(2,1)} %bitcast.91, bf16[1,128,4096]{2,1,0:T(8,128)(2,1)} %bitcast.92), kind=kLoop, calls=%fused_computation.27 | loop fusion | flops 1048576 | bytes 4194304 | tf_op jit(solution)/shard_map/stack | solution.py:50
  3.1 4.7 %copy.52 = bf16[2,128,4096]{1,0,2:T(2,128)(2,1)S(1)} copy(bf16[2,128,4096]{2,1,0:T(8,128)(2,1)} %pad_maximum_fusion.1) | data formatting | bytes 4194304 | tf_op jit(solution)/shard_map/stack | solution.py:50
  7.8 54.3 %all_to_all.53 = bf16[2,128,4096]{1,0,2:T(2,128)(2,1)S(1)} all-to-all(bf16[2,128,4096]{1,0,2:T(2,128)(2,1)S(1)} %copy.52), channel_id=1, replica_groups=mesh['blk'=4,'head'=8] {'head'}, dimensions={2} | all-to-all | bytes 4194304 | tf_op jit(solution)/shard_map/all_to_all | solution.py:49
  62.4 2.6 copy.54
  65.0 1.2 collective-permute-start
  66.3 1.2 collective-permute-start.1
  67.4 1.1 copy.76
  68.5 5.1 %all-to-all-start.1 = ((bf16[128,8,512]{2,0,1:T(8,128)(2,1)}), bf16[128,8,512]{2,0,1:T(8,128)(2,1)S(1)}, u32[]{:S(2)}, u32[]{:S(2)}) async-start(bf16[128,8,512]{2,0,1:T(8,128)(2,1)} %bitcast.58), calls=%async_computation.1 | async-start | bytes 2097152 | tf_op jit(solution)/shard_map/all_to_all | solution.py:48
  73.6 0.7 and_select_fusion
  74.3 25.1 %all-to-all-done.1 = bf16[128,8,512]{2,0,1:T(8,128)(2,1)S(1)} async-done(((bf16[128,8,512]{2,0,1:T(8,128)(2,1)}), bf16[128,8,512]{2,0,1:T(8,128)(2,1)S(1)}, u32[]{:S(2)}, u32[]{:S(2)}) %all-to-all-start.1) | async-done | bytes 1048608 | tf_op jit(solution)/shard_map/all_to_all | solution.py:48
  99.7 12.7 %collective-permute-done = bf16[2,1024,512]{2,1,0:T(8,128)(2,1)} collective-permute-done((bf16[2,1024,512]{2,1,0:T(8,128)(2,1)}, bf16[2,1024,512]{2,1,0:T(8,128)(2,1)}, u32[]{:S(2)}, u32[]{:S(2)}) %collective-permute-start) | collective-permute-done | bytes 2097184 | tf_op jit(solution)/shard_map/ppermute | solution.py:14
  112.3 45.0 %collective-permute-done.1 = bf16[2,1024,512]{2,1,0:T(8,128)(2,1)} collective-permute-done((bf16[2,1024,512]{2,1,0:T(8,128)(2,1)}, bf16[2,1024,512]{2,1,0:T(8,128)(2,1)}, u32[]{:S(2)}, u32[]{:S(2)}) %collective-permute-start.1) | collective-permute-done | bytes 2097184 | tf_op jit(solution)/shard_map/ppermute | solution.py:14
  157.3 5.9 %pad_maximum_fusion = bf16[2,3072,512]{2,1,0:T(8,128)(2,1)} fusion(bf16[2,1024,512]{2,1,0:T(8,128)(2,1)} %collective-permute-done.1, bf16[2,1024,512]{2,1,0:T(8,128)(2,1)} %bitcast.85, bf16[2,1024,512]{2,1,0:T(8,128)(2,1)} %collective-permute-done), kind=kLoop, calls=%fused_computation.26 | loop fusion | flops 18874368 | bytes 12582912 | tf_op jit(solution)/shard_map/concatenate | solution.py:54
  163.2 9.7 %reshape.50 = bf16[2,6,512,4,128]{4,3,2,1,0:T(4,128)(2,1)} reshape(bf16[2,3072,512]{2,1,0:T(8,128)(2,1)} %pad_maximum_fusion) | data formatting | bytes 12582912 | tf_op jit(solution)/shard_map/reshape | solution.py:23
  173.0 7.1 %copy.56 = bf16[2,6,512,4,128]{4,2,3,1,0:T(8,128)(2,1)} copy(bf16[2,6,512,4,128]{4,3,2,1,0:T(4,128)(2,1)} %reshape.50) | data formatting | bytes 12582912
  180.1 86.5 %while.11 = (s32[]{:T(128)}, bf16[2,512,512]{2,1,0:T(8,128)(2,1)S(1)}, s32[2,6]{1,0:T(2,128)S(1)}, bf16[2,6,512,4,128]{4,2,3,1,0:T(8,128)(2,1)}, s32[2]{0:T(128)...) while((s32[]{:T(128)}, bf16[2,512,512]{2,1,0:T(8,128)(2,1)S(1)}, s32[2,6]{1,0:T(2,128)S(1)}, ...), condition=%wide.region_3.4_spmd.clone, body=%wide.region_0.3_spmd.clone.sunk | while | flops 3290952704 | bytes 111195344 | solution.py:42
  180.1 6.8 %gather_fusion = bf16[6,2,512,4,128]{4,2,3,1,0:T(8,128)(2,1)} fusion(bf16[2,6,512,4,128]{4,2,3,1,0:T(8,128)(2,1)} %get-tuple-element.159, s32[1024]{0:T(1024)S(1)} %pad_clamp_fusion.2), kind=kCustom, calls=%fused_computation.clone.clone.1 | custom fusion | bytes 12582936 | tf_op jit(solution)/shard_map/while/body/eval_jaxpr/gather | solution.py:28
  186.9 3.2 %copy.81 = bf16[6,2,512,4,128]{4,2,0,3,1:T(8,128)(2,1)S(1)} copy(bf16[6,2,512,4,128]{4,2,3,1,0:T(8,128)(2,1)} %gather_fusion) | data formatting | bytes 12582912 | tf_op jit(solution)/shard_map/while/body/eval_jaxpr/gather | solution.py:28
  190.7 0.6 iota_compare_fusion.2
  191.5 10.1 %select_reduce_fusion.2 = (f32[4,512]{1,0:T(4,128)S(1)}, f32[4,512,6,512]{1,3,2,0:T(8,128)}) fusion(pred[6]{0:T(512)(128)(4,1)S(1)} %iota_compare_fusion.2, bf16[2,6,512,4,128]{4,2,1,3,0:T(8,128)(2,1)S(1)} %bitcast.79, bf16[1,512,4,128]{3,2,1,0:T(4,128)(2,1)S(1)} %constant_dynamic-slice_fusion.3), kind=kOutput, calls=%fused_computation.3.clone.1 | convolution fusion | flops 1629485056 | bytes 28844544 | tf_op jit(solution)/shard_map/while/body/eval_jaxpr/qhd,jkhd->hqjk/dot_general | solution.py:31
  201.6 10.9 %fusion.28 = f32[4,512]{1,0:T(4,128)S(1)} fusion(f32[4,512,6,512]{1,3,2,0:T(8,128)} %get-tuple-element.140, f32[4,512]{1,0:T(4,128)S(1)} %get-tuple-element.141, pred[6]{0:T(512)(128)(4,1)S(1)} %iota_compare_fusion.2), kind=kLoop, calls=%fused_computation.4.clone.1 | loop fusion | flops 25163776 | bytes 25182214 | tf_op jit(solution)/shard_map/while/body/eval_jaxpr/reduce_sum | solution.py:36
  212.5 10.6 %fusion.29 = bf16[512,4,128]{0,2,1:T(8,128)(2,1)S(1)} fusion(f32[4,512,6,512]{1,3,2,0:T(8,128)} %get-tuple-element.140, f32[4,512]{1,0:T(4,128)S(1)} %get-tuple-element.141, pred[6]{0:T(512)(128)(4,1)S(1)} %iota_compare_fusion.2, bf16[2,6,512,4,128]{4,2,1,3,0:T(8,128)(2,1)S(1)} %bitcast.80, f32[512,4]{0,1:T(4,128)S(1)} %bitcast.93), kind=kOutput, calls=%fused_computation.14.clone.1 | convolution fusion | flops 1636302848 | bytes 28852736 | tf_op jit(solution)/shard_map/while/body/eval_jaxpr/hqjk,jkhd->qhd/dot_general | solution.py:38
  223.4 6.8 %gather_fusion = bf16[6,2,512,4,128]{4,2,3,1,0:T(8,128)(2,1)} fusion(bf16[2,6,512,4,128]{4,2,3,1,0:T(8,128)(2,1)} %get-tuple-element.159, s32[1024]{0:T(1024)S(1)} %pad_clamp_fusion.2), kind=kCustom, calls=%fused_computation.clone.clone.1 | custom fusion | bytes 12582936 | tf_op jit(solution)/shard_map/while/body/eval_jaxpr/gather | solution.py:28
  230.2 3.2 %copy.81 = bf16[6,2,512,4,128]{4,2,0,3,1:T(8,128)(2,1)S(1)} copy(bf16[6,2,512,4,128]{4,2,3,1,0:T(8,128)(2,1)} %gather_fusion) | data formatting | bytes 12582912 | tf_op jit(solution)/shard_map/while/body/eval_jaxpr/gather | solution.py:28
  233.4 0.6 dynamic_slice.37
  234.0 0.6 iota_compare_fusion.2
  234.8 10.1 %select_reduce_fusion.2 = (f32[4,512]{1,0:T(4,128)S(1)}, f32[4,512,6,512]{1,3,2,0:T(8,128)}) fusion(pred[6]{0:T(512)(128)(4,1)S(1)} %iota_compare_fusion.2, bf16[2,6,512,4,128]{4,2,1,3,0:T(8,128)(2,1)S(1)} %bitcast.79, bf16[1,512,4,128]{3,2,1,0:T(4,128)(2,1)S(1)} %constant_dynamic-slice_fusion.3), kind=kOutput, calls=%fused_computation.3.clone.1 | convolution fusion | flops 1629485056 | bytes 28844544 | tf_op jit(solution)/shard_map/while/body/eval_jaxpr/qhd,jkhd->hqjk/dot_general | solution.py:31
  244.9 10.9 %fusion.28 = f32[4,512]{1,0:T(4,128)S(1)} fusion(f32[4,512,6,512]{1,3,2,0:T(8,128)} %get-tuple-element.140, f32[4,512]{1,0:T(4,128)S(1)} %get-tuple-element.141, pred[6]{0:T(512)(128)(4,1)S(1)} %iota_compare_fusion.2), kind=kLoop, calls=%fused_computation.4.clone.1 | loop fusion | flops 25163776 | bytes 25182214 | tf_op jit(solution)/shard_map/while/body/eval_jaxpr/reduce_sum | solution.py:36
  255.7 10.6 %fusion.29 = bf16[512,4,128]{0,2,1:T(8,128)(2,1)S(1)} fusion(f32[4,512,6,512]{1,3,2,0:T(8,128)} %get-tuple-element.140, f32[4,512]{1,0:T(4,128)S(1)} %get-tuple-element.141, pred[6]{0:T(512)(128)(4,1)S(1)} %iota_compare_fusion.2, bf16[2,6,512,4,128]{4,2,1,3,0:T(8,128)(2,1)S(1)} %bitcast.80, f32[512,4]{0,1:T(4,128)S(1)} %bitcast.93), kind=kOutput, calls=%fused_computation.14.clone.1 | convolution fusion | flops 1636302848 | bytes 28852736 | tf_op jit(solution)/shard_map/while/body/eval_jaxpr/hqjk,jkhd->qhd/dot_general | solution.py:38
  266.6 30.4 %all_to_all.54 = bf16[8,128,512]{2,1,0:T(8,128)(2,1)S(1)} all-to-all(bf16[8,128,512]{2,1,0:T(8,128)(2,1)S(1)} %bitcast.90), channel_id=1, replica_groups=mesh['blk'=4,'head'=8] {'head'}, dimensions={0} | all-to-all | bytes 2097152 | tf_op jit(solution)/shard_map/all_to_all | solution.py:62
  297.1 0.7 copy.59
  297.7 1.3 copy.60
  (19 shorter events, 2.1 us)
Async XLA Ops:
  7.8 59.6 %copy-start = (bf16[128,4096]{1,0:T(8,128)(2,1)S(1)}, bf16[128,4096]{1,0:T(8,128)(2,1)}, u32[]{:S(2)}) copy-start(bf16[128,4096]{1,0:T(8,128)(2,1)} %param.7) | copy-start | bytes 3145732
  62.1 11.4 %copy-start.1 = (s32[8]{0:T(128)S(1)}, s32[8]{0:T(128)}, u32[]{:S(2)}) copy-start(s32[8]{0:T(128)} %param.11) | copy-start | bytes 100
  65.0 47.3 %collective-permute-start = (bf16[2,1024,512]{2,1,0:T(8,128)(2,1)}, bf16[2,1024,512]{2,1,0:T(8,128)(2,1)}, u32[]{:S(2)}, u32[]{:S(2)}) collective-permute-start(bf16[2,1024,512]{2,1,0:T(8,128)(2,1)} %bitcast.83), channel_id=1, source_target_pairs={{0,8},{8,16},{16,24},{24,0},{1,9},{9,17},{17,25},{25,1},{2,10},{10... | collective-permute-start | bytes 6291464 | tf_op jit(solution)/shard_map/ppermute | solution.py:14
  66.3 91.1 %collective-permute-start.1 = (bf16[2,1024,512]{2,1,0:T(8,128)(2,1)}, bf16[2,1024,512]{2,1,0:T(8,128)(2,1)}, u32[]{:S(2)}, u32[]{:S(2)}) collective-permute-start(bf16[2,1024,512]{2,1,0:T(8,128)(2,1)} %bitcast.84), channel_id=1, source_target_pairs={{0,24},{8,0},{16,8},{24,16},{1,25},{9,1},{17,9},{25,17},{2,26},{10... | collective-permute-start | bytes 6291464 | tf_op jit(solution)/shard_map/ppermute | solution.py:14
  68.5 30.9 %all-to-all-start.1 = ((bf16[128,8,512]{2,0,1:T(8,128)(2,1)}), bf16[128,8,512]{2,0,1:T(8,128)(2,1)S(1)}, u32[]{:S(2)}, u32[]{:S(2)}) async-start(bf16[128,8,512]{2,0,1:T(8,128)(2,1)} %bitcast.58), calls=%async_computation.1 | async-start | bytes 2097152 | tf_op jit(solution)/shard_map/all_to_all | solution.py:48
where the time goes:
time: 301 us; the launch traced here: 299 us
  blocking collectives  84.8 us (28%)
  waiting for transfers between devices  82.7 us (27%)
  local copies, waits for them, and re-layouts  49.9 us (17%)
  matrix products  41.3 us (14%)
  other arithmetic  32.7 us (11%)
  starting transfers between devices  7.43 us (2%)
    ppermute x2, waiting for transfers between devices, from_behind(): return lax.ppermute(value, axis, pairs)  57.7 us
    all_to_all x1, blocking collectives, local(): lax.all_to_all(jnp.stack([keys, values]), 'head', split_axis=2, concat_ax...  54.3 us
    all_to_all x1, blocking collectives, local(): lax.all_to_all(attended_rows, 'head', split_axis=0, concat_axis=1, tiled=...  30.4 us
    all_to_all x1, waiting for transfers between devices, local(): lax.all_to_all(queries, 'head', split_axis=1, concat_axis=0, tiled=True)  25.1 us
    reduce_sum x2, other arithmetic, attend_block(): total = jnp.sum(expo, axis=(2, 3))  21.7 us
    dot_general x2, matrix products, attend_block(): jnp.einsum('hqjk,jkhd->qhd', weights, chosen[1], preferred_element_type=j...  21.2 us
    dot_general x2, matrix products, attend_block(): jnp.einsum('qhd,jkhd->hqjk', query_block, chosen[0], preferred_element_ty...  20.1 us
    gather x4, local copies, waits for them, and re-layouts, attend_block(): chosen = pair_blocks[:, listed]  20 us
  transfers between devices with their start and end apart: 3, of which 3 were waited for; matrix products, arithmetic and copies ran while one was open for 1% of the time, Pallas kernels for 0%

commit v1 on v0

--- a/solution.py
+++ b/solution.py
@@ -1,6 +1,11 @@
+import functools
+import math
+
 import jax
 import jax.numpy as jnp
 from jax import lax
+from jax.experimental import pallas as pl
+from jax.experimental.pallas import tpu as pltpu
 from jax.sharding import PartitionSpec as P
 
 HD = 128
@@ -62,7 +67,211 @@
     return lax.all_to_all(attended_rows, "head", split_axis=0, concat_axis=1, tiled=True)
 
 
+MESH = pl.DeviceIdType.MESH
+QTILE = 256
+
+
+def head_kernel(
+    cycle, group, blocks_here, q_ref, k_ref, v_ref, bias_ref, out_ref,
+    q_all, k_all, v_all, o_all, scores, weights, total,
+    send_sem, recv_sem, own_sem, out_send_sem, out_recv_sem, out_own_sem,
+):
+    count = cycle * group
+    rows = q_ref.shape[0]
+    my_blk = lax.axis_index("blk")
+    my_head = lax.axis_index("head")
+    me = my_blk * group + my_head
+    span = 3 * blocks_here
+    blocks = cycle * blocks_here
+    exponent = HD ** (-0.5) * math.log2(math.e)
+    inputs = ((k_ref, k_all), (q_ref, q_all), (v_ref, v_all))
+
+    def target(step):
+        blk = lax.rem(my_blk + lax.div(step, group), cycle)
+        head = lax.rem(my_head + lax.rem(step, group), group)
+        return blk, head
+
+    def columns(device):
+        return pl.ds(pl.multiple_of(device * HD, HD), HD)
+
+    def rows_of(device):
+        return pl.ds(pl.multiple_of(device * rows, rows), rows)
+
+    barrier = pltpu.get_barrier_semaphore()
+
+    def greet(step, carry):
+        pl.semaphore_signal(barrier, inc=1, device_id=target(step), device_id_type=MESH)
+        return carry
+
+    lax.fori_loop(1, count, greet, 0)
+    pl.semaphore_wait(barrier, count - 1)
+
+    for index, (source, gathered) in enumerate(inputs):
+
+        def send(step, carry):
+            blk, head = target(step)
+            pltpu.make_async_remote_copy(
+                src_ref=source.at[:, columns(blk * group + head)],
+                dst_ref=gathered.at[rows_of(me), :],
+                send_sem=send_sem.at[index],
+                recv_sem=recv_sem.at[index],
+                device_id=(blk, head),
+                device_id_type=MESH,
+            ).start()
+            return carry
+
+        lax.fori_loop(1, count, send, 0)
+        pltpu.make_async_copy(
+            source.at[:, columns(me)], gathered.at[rows_of(me), :], own_sem.at[index]
+        ).start()
+
+    def arrived(index):
+        source, gathered = inputs[index]
+        pltpu.make_async_copy(
+            source.at[:, columns(me)], gathered.at[rows_of(me), :], own_sem.at[index]
+        ).wait()
+        others = gathered.at[pl.ds(0, (count - 1) * rows), :]
+        pltpu.make_async_copy(others, others, recv_sem.at[index]).wait()
+
+    def key_rows(block, j):
+        shard = lax.div(block, blocks_here)
+        chosen = lax.rem((shard + cycle - 1) * blocks_here + j, blocks)
+        return pl.ds(pl.multiple_of(chosen * BLOCK, BLOCK), BLOCK)
+
+    arrived(0)
+    arrived(1)
+    tiles = BLOCK // QTILE
+
+    def weigh(step, carry):
+        block = lax.div(step, tiles)
+        here = pl.ds(pl.multiple_of(step * QTILE, QTILE), QTILE)
+        query = q_all[here, :]
+        top = None
+        for j in range(span):
+            part = lax.dot_general(
+                query, k_all[key_rows(block, j), :], (((1,), (1,)), ((), ())),
+                preferred_element_type=jnp.float32,
+            )
+            scores[j] = part
+            part_top = jnp.max(part, axis=1, keepdims=True) + bias_ref[block, j]
+            top = part_top if top is None else jnp.maximum(top, part_top)
+        shift = top * exponent
+        amount = None
+        for j in range(span):
+            expo = jnp.exp2(scores[j] * exponent + (bias_ref[block, j] - shift))
+            weights[here, j * BLOCK:(j + 1) * BLOCK] = expo.astype(jnp.bfloat16)
+            part_sum = jnp.sum(expo, axis=1, keepdims=True)
+            amount = part_sum if amount is None else amount + part_sum
+        total[here, :] = amount
+        return carry
+
+    lax.fori_loop(0, blocks * tiles, weigh, 0)
+    arrived(2)
+
+    owners = BLOCK // rows
+    my_block = lax.div(me, owners)
+    half = blocks // 2
+
+    def finish(step, carry):
+        offset = lax.rem(2 * step + 1 + lax.div(step, half), blocks)
+        block = lax.rem(my_block + offset, blocks)
+
+        def mix(tile, inner):
+            start = block * BLOCK + tile * QTILE
+            here = pl.ds(pl.multiple_of(start, QTILE), QTILE)
+            mixed = None
+            for j in range(span):
+                part = jnp.dot(
+                    weights[here, j * BLOCK:(j + 1) * BLOCK], v_all[key_rows(block, j), :],
+                    preferred_element_type=jnp.float32,
+                )
+                mixed = part if mixed is None else mixed + part
+            o_all[here, :] = (mixed / total[here, :]).astype(jnp.bfloat16)
+            return inner
+
+        lax.fori_loop(0, tiles, mix, 0)
+
+        def give(owner, inner):
+            device = block * owners + owner
+
+            @pl.when(device != me)
+            def _():
+                pltpu.make_async_remote_copy(
+                    src_ref=o_all.at[rows_of(device), :],
+                    dst_ref=out_ref.at[:, columns(me)],
+                    send_sem=out_send_sem,
+                    recv_sem=out_recv_sem,
+                    device_id=(lax.div(device, group), lax.rem(device, group)),
+                    device_id_type=MESH,
+                ).start()
+
+            @pl.when(device == me)
+            def _():
+                pltpu.make_async_copy(
+                    o_all.at[rows_of(device), :], out_ref.at[:, columns(me)], out_own_sem
+                ).start()
+
+            return inner
+
+        lax.fori_loop(0, owners, give, 0)
+        return carry
+
+    lax.fori_loop(0, blocks, finish, 0)
+
+    pltpu.make_async_copy(
+        o_all.at[rows_of(me), :], out_ref.at[:, columns(me)], out_own_sem
+    ).wait()
+    others = o_all.at[pl.ds(0, (count - 1) * rows), :]
+    for index in range(3):
+        pltpu.make_async_copy(others, others, send_sem.at[index]).wait()
+    pltpu.make_async_copy(others, others, out_send_sem).wait()
+    pltpu.make_async_copy(others, others, out_recv_sem).wait()
+
+
+def local_heads(cycle, group, queries, keys, values, key_blocks, counts):
+    rows, width = queries.shape
+    tokens = rows * cycle * group
+    blocks = tokens // BLOCK
+    blocks_here = blocks // cycle
+    span = 3 * blocks_here
+    block_ids = jnp.arange(blocks, dtype=jnp.int32)
+    first = (block_ids // blocks_here + cycle - 1) * blocks_here
+    offered = (first[:, None] + jnp.arange(span, dtype=jnp.int32)[None, :]) % blocks
+    used = jnp.arange(key_blocks.shape[1], dtype=jnp.int32)[None, :] < counts[:, None]
+    listed = (key_blocks[:, None, :] == offered[:, :, None]) & used[:, None, :]
+    bias = jnp.where(jnp.any(listed, axis=2), 0.0, -jnp.inf).astype(jnp.float32)
+    whole = pltpu.VMEM((tokens, HD), jnp.bfloat16)
+    return pl.pallas_call(
+        functools.partial(head_kernel, cycle, group, blocks_here),
+        out_shape=jax.ShapeDtypeStruct((rows, width), jnp.bfloat16),
+        in_specs=[pl.BlockSpec(memory_space=pl.ANY)] * 3
+        + [pl.BlockSpec(memory_space=pltpu.SMEM)],
+        out_specs=pl.BlockSpec(memory_space=pl.ANY),
+        scratch_shapes=[
+            whole, whole, whole, whole,
+            pltpu.VMEM((span, QTILE, BLOCK), jnp.float32),
+            pltpu.VMEM((tokens, span * BLOCK), jnp.bfloat16),
+            pltpu.VMEM((tokens, 1), jnp.float32),
+            pltpu.SemaphoreType.DMA((3,)),
+            pltpu.SemaphoreType.DMA((3,)),
+            pltpu.SemaphoreType.DMA((3,)),
+            pltpu.SemaphoreType.DMA,
+            pltpu.SemaphoreType.DMA,
+            pltpu.SemaphoreType.DMA,
+        ],
+        compiler_params=pltpu.CompilerParams(
+            collective_id=0, has_side_effects=True, vmem_limit_bytes=56 * 2**20
+        ),
+        cost_estimate=pl.CostEstimate(
+            flops=4 * tokens * span * BLOCK * HD,
+            bytes_accessed=8 * rows * width,
+            transcendentals=tokens * span * BLOCK,
+        ),
+    )(queries, keys, values, bias)
+
+
 def solution(mesh):
+    cycle, group = mesh.shape["blk"], mesh.shape["head"]
     placed = (
         P(("blk", "head"), None),
         P(("blk", "head"), None),
@@ -70,6 +279,13 @@
         P(),
         P(),
     )
+    one_head_each = cycle * group * HD
+
+    def chosen(queries, *others):
+        if queries.shape[1] == one_head_each and cycle >= 3:
+            return local_heads(cycle, group, queries, *others)
+        return local(queries, *others)
+
     return jax.shard_map(
-        local, mesh=mesh, in_specs=placed, out_specs=P(("blk", "head"), None), check_vma=False
+        chosen, mesh=mesh, in_specs=placed, out_specs=P(("blk", "head"), None), check_vma=False
     )

time: 301 us -> 114 us (0.38)
  Pallas kernels: 0 us -> 109 us
  blocking collectives: 84.8 us -> 0 us
  waiting for transfers between devices: 82.7 us -> 0 us
  local copies, waits for them, and re-layouts: 49.9 us -> 3.04 us
  matrix products: 41.3 us -> 0 us
  other arithmetic: 32.7 us -> 0.95 us
  starting transfers between devices: 7.43 us -> 0 us
    pallas_call x0 -> x1, Pallas kernels: none -> 109 us  [local_heads(): pl.pallas_call(functools.partial(head_kernel, cycle, group, blocks_here),...]
    all_to_all x2 -> x0, blocking collectives: 84.8 us -> none  [the longest x1 54.3 us: local(): lax.all_to_all(jnp.stack([keys, values]), 'head', split_axis=2, concat_ax...]
    ppermute x2 -> x0, waiting for transfers between devices: 57.7 us -> none  [from_behind(): return lax.ppermute(value, axis, pairs)]
    dot_general x4 -> x0, matrix products: 41.3 us -> none  [the longest x2 21.2 us: attend_block(): jnp.einsum('hqjk,jkhd->qhd', weights, chosen[1], preferred_element_type=j...]
    all_to_all x1 -> x0, waiting for transfers between devices: 25.1 us -> none  [local(): lax.all_to_all(queries, 'head', split_axis=1, concat_axis=0, tiled=True)]
    reduce_sum x2 -> x0, other arithmetic: 21.7 us -> none  [attend_block(): total = jnp.sum(expo, axis=(2, 3))]
    gather x4 -> x0, local copies, waits for them, and re-layouts: 20 us -> none  [attend_block(): chosen = pair_blocks[:, listed]]
    reshape x2 -> x0, local copies, waits for them, and re-layouts: 10 us -> none  [the longest x1 9.74 us: attend_shard(): pair_blocks = context.reshape(2, 3 * blocks_here, BLOCK, heads_local, HD)]
  transfers between devices with their start and end apart: 3 -> 0, of which waited for: 3 -> 0; matrix products, arithmetic and copies ran while one was open for 1% -> 0% of each run, Pallas kernels for 0% -> 0%
where the time goes in v1:
time: 114 us; the launch traced here: 113 us
  Pallas kernels  109 us (96%)
  local copies, waits for them, and re-layouts  3.04 us (3%)
    pallas_call x1, Pallas kernels, local_heads(): pl.pallas_call(functools.partial(head_kernel, cycle, group, blocks_here),...  109 us
    unnamed x5, local copies, waits for them, and re-layouts  2.94 us

profile of v1, /device:TPU:1, one launch (start us, length us, event | category | flops | bytes accessed | tf_op | source)
XLA Modules:
  0.0 113.0 jit_solution(13355484189082075575)
XLA Ops:
  0.0 0.0 copy-start.1
  0.0 0.0 copy-start
  0.0 0.6 copy-done.1
  0.7 0.1 iota_compare_fusion
  0.7 0.0 copy-done
  0.7 0.3 and_reduce_fusion
  1.0 0.1 copy.6
  1.1 0.6 broadcast_select_fusion.bias_ref
  1.7 109.0 %shard_map.55 = bf16[128,4096]{1,0:T(8,128)(2,1)} custom-call(bf16[128,4096]{1,0:T(8,128)(2,1)} %q_ref.1, bf16[128,4096]{1,0:T(8,128)(2,1)} %k_ref.1, bf16[128,4096]{1,0:T(8,128)(2,1)} %v_ref.1, f32[8,6]{1,0:T(8,128)} %broadcast_select_fusion.bias_ref), custom_call_target="tpu_custom_call" | custom-call | flops 6442450944 | bytes 4194304 | tf_op jit(solution)/shard_map/pallas_call | solution.py:244
  110.7 2.3 %copy.8 = bf16[128,4096]{1,0:T(8,128)(2,1)} copy(bf16[128,4096]{1,0:T(8,128)(2,1)} %shard_map.55) | data formatting | bytes 2097152
  (2 shorter events, 0.0 us)
Async XLA Ops:
  0.0 0.7 copy-start.1
  0.0 0.7 copy-start

commit v2 on v1

--- a/solution.py
+++ b/solution.py
@@ -72,9 +72,9 @@
 
 
 def head_kernel(
-    cycle, group, blocks_here, q_ref, k_ref, v_ref, bias_ref, out_ref,
-    q_all, k_all, v_all, o_all, scores, weights, total,
-    send_sem, recv_sem, own_sem, out_send_sem, out_recv_sem, out_own_sem,
+    cycle, group, blocks_here, q_ref, k_ref, v_ref, lists_ref, counts_ref, out_ref,
+    q_all, k_all, v_all, o_all, scores, weights, total, lists, amounts, bias_ref,
+    send_sem, recv_sem, own_sem, list_sem, out_send_sem, out_recv_sem, out_own_sem,
 ):
     count = cycle * group
     rows = q_ref.shape[0]
@@ -106,7 +106,8 @@
     lax.fori_loop(1, count, greet, 0)
     pl.semaphore_wait(barrier, count - 1)
 
-    for index, (source, gathered) in enumerate(inputs):
+    def send_all(index):
+        source, gathered = inputs[index]
 
         def send(step, carry):
             blk, head = target(step)
@@ -114,32 +115,63 @@
                 src_ref=source.at[:, columns(blk * group + head)],
                 dst_ref=gathered.at[rows_of(me), :],
                 send_sem=send_sem.at[index],
-                recv_sem=recv_sem.at[index],
+                recv_sem=recv_sem.at[index, lax.div(step, group)],
                 device_id=(blk, head),
                 device_id_type=MESH,
             ).start()
             return carry
 
         lax.fori_loop(1, count, send, 0)
-        pltpu.make_async_copy(
+
+    def own_copy(index):
+        source, gathered = inputs[index]
+        return pltpu.make_async_copy(
             source.at[:, columns(me)], gathered.at[rows_of(me), :], own_sem.at[index]
-        ).start()
-
-    def arrived(index):
-        source, gathered = inputs[index]
-        pltpu.make_async_copy(
-            source.at[:, columns(me)], gathered.at[rows_of(me), :], own_sem.at[index]
-        ).wait()
-        others = gathered.at[pl.ds(0, (count - 1) * rows), :]
-        pltpu.make_async_copy(others, others, recv_sem.at[index]).wait()
+        )
+
+    def arrived(index, back):
+        gathered = inputs[index][1]
+        if back == 0:
+            own_copy(index).wait()
+        senders = group - 1 if back == 0 else group
+        part = gathered.at[pl.ds(0, senders * rows), :]
+        pltpu.make_async_copy(part, part, recv_sem.at[index, back]).wait()
+
+    def key_block(block, j):
+        shard = lax.div(block, blocks_here)
+        return lax.rem((shard + cycle - 1) * blocks_here + j, blocks)
 
     def key_rows(block, j):
-        shard = lax.div(block, blocks_here)
-        chosen = lax.rem((shard + cycle - 1) * blocks_here + j, blocks)
-        return pl.ds(pl.multiple_of(chosen * BLOCK, BLOCK), BLOCK)
-
-    arrived(0)
-    arrived(1)
+        return pl.ds(pl.multiple_of(key_block(block, j) * BLOCK, BLOCK), BLOCK)
+
+    send_all(0)
+    send_all(1)
+    for index in range(3):
+        own_copy(index).start()
+    list_copies = (
+        pltpu.make_async_copy(lists_ref, lists, list_sem.at[0]),
+        pltpu.make_async_copy(counts_ref, amounts, list_sem.at[1]),
+    )
+    for copy in list_copies:
+        copy.start()
+    for copy in list_copies:
+        copy.wait()
+
+    def mark(block, carry):
+        for j in range(span):
+            offered = key_block(block, j)
+            hits = jnp.int32(0)
+            for slot in range(MAXB):
+                same = lists[block, slot] == offered
+                hits += jnp.where(same & (slot < amounts[block]), 1, 0)
+            bias_ref[block, j] = jnp.where(hits > 0, 0.0, -jnp.inf)
+        return carry
+
+    lax.fori_loop(0, blocks, mark, 0)
+
+    for back in range(cycle):
+        arrived(0, back)
+    send_all(2)
     tiles = BLOCK // QTILE
 
     def weigh(step, carry):
@@ -165,16 +197,21 @@
         total[here, :] = amount
         return carry
 
-    lax.fori_loop(0, blocks * tiles, weigh, 0)
-    arrived(2)
-
-    owners = BLOCK // rows
-    my_block = lax.div(me, owners)
-    half = blocks // 2
-
-    def finish(step, carry):
-        offset = lax.rem(2 * step + 1 + lax.div(step, half), blocks)
-        block = lax.rem(my_block + offset, blocks)
+    per_shard = blocks_here * tiles
+    for back in range(cycle):
+        arrived(1, back)
+        first = lax.rem(my_blk + cycle - back, cycle) * per_shard
+
+        def weigh_here(step, carry):
+            return weigh(first + step, carry)
+
+        lax.fori_loop(0, per_shard, weigh_here, 0)
+
+    owners = QTILE // rows
+    my_place = lax.rem(lax.div(me * rows, BLOCK), blocks_here)
+
+    def finish(shard, turn):
+        block = shard * blocks_here + lax.rem(my_place + 1 + turn, blocks_here)
 
         def mix(tile, inner):
             start = block * BLOCK + tile * QTILE
@@ -187,36 +224,50 @@
                 )
                 mixed = part if mixed is None else mixed + part
             o_all[here, :] = (mixed / total[here, :]).astype(jnp.bfloat16)
-            return inner
+
+            def give(owner, carry):
+                device = (block * tiles + tile) * owners + owner
+
+                @pl.when(device != me)
+                def _():
+                    pltpu.make_async_remote_copy(
+                        src_ref=o_all.at[rows_of(device), :],
+                        dst_ref=out_ref.at[:, columns(me)],
+                        send_sem=out_send_sem,
+                        recv_sem=out_recv_sem,
+                        device_id=(lax.div(device, group), lax.rem(device, group)),
+                        device_id_type=MESH,
+                    ).start()
+
+                @pl.when(device == me)
+                def _():
+                    pltpu.make_async_copy(
+                        o_all.at[rows_of(device), :], out_ref.at[:, columns(me)], out_own_sem
+                    ).start()
+
+                return carry
+
+            return lax.fori_loop(0, owners, give, inner)
 
         lax.fori_loop(0, tiles, mix, 0)
 
-        def give(owner, inner):
-            device = block * owners + owner
-
-            @pl.when(device != me)
-            def _():
-                pltpu.make_async_remote_copy(
-                    src_ref=o_all.at[rows_of(device), :],
-                    dst_ref=out_ref.at[:, columns(me)],
-                    send_sem=out_send_sem,
-                    recv_sem=out_recv_sem,
-                    device_id=(lax.div(device, group), lax.rem(device, group)),
-                    device_id_type=MESH,
-                ).start()
-
-            @pl.when(device == me)
-            def _():
-                pltpu.make_async_copy(
-                    o_all.at[rows_of(device), :], out_ref.at[:, columns(me)], out_own_sem
-                ).start()
-
-            return inner
-
-        lax.fori_loop(0, owners, give, 0)
-        return carry
-
-    lax.fori_loop(0, blocks, finish, 0)
+    for back in range(3):
+        arrived(2, back)
+
+    def finish_previous(turn, carry):
+        finish(lax.rem(my_blk + cycle - 1, cycle), turn)
+        return carry
+
+    lax.fori_loop(0, blocks_here, finish_previous, 0)
+    for back in range(3, cycle):
+        arrived(2, back)
+
+    def finish_rest(step, carry):
+        ahead = lax.rem(lax.rem(step, cycle - 1) + 1, cycle - 1)
+        finish(lax.rem(my_blk + ahead, cycle), lax.div(step, cycle - 1))
+        return carry
+
+    lax.fori_loop(0, blocks_here * (cycle - 1), finish_rest, 0)
 
     pltpu.make_async_copy(
         o_all.at[rows_of(me), :], out_ref.at[:, columns(me)], out_own_sem
@@ -234,27 +285,25 @@
     blocks = tokens // BLOCK
     blocks_here = blocks // cycle
     span = 3 * blocks_here
-    block_ids = jnp.arange(blocks, dtype=jnp.int32)
-    first = (block_ids // blocks_here + cycle - 1) * blocks_here
-    offered = (first[:, None] + jnp.arange(span, dtype=jnp.int32)[None, :]) % blocks
-    used = jnp.arange(key_blocks.shape[1], dtype=jnp.int32)[None, :] < counts[:, None]
-    listed = (key_blocks[:, None, :] == offered[:, :, None]) & used[:, None, :]
-    bias = jnp.where(jnp.any(listed, axis=2), 0.0, -jnp.inf).astype(jnp.float32)
+    span = 3 * blocks_here
     whole = pltpu.VMEM((tokens, HD), jnp.bfloat16)
     return pl.pallas_call(
         functools.partial(head_kernel, cycle, group, blocks_here),
         out_shape=jax.ShapeDtypeStruct((rows, width), jnp.bfloat16),
-        in_specs=[pl.BlockSpec(memory_space=pl.ANY)] * 3
-        + [pl.BlockSpec(memory_space=pltpu.SMEM)],
+        in_specs=[pl.BlockSpec(memory_space=pl.ANY)] * 5,
         out_specs=pl.BlockSpec(memory_space=pl.ANY),
         scratch_shapes=[
             whole, whole, whole, whole,
             pltpu.VMEM((span, QTILE, BLOCK), jnp.float32),
             pltpu.VMEM((tokens, span * BLOCK), jnp.bfloat16),
             pltpu.VMEM((tokens, 1), jnp.float32),
+            pltpu.SMEM(key_blocks.shape, jnp.int32),
+            pltpu.SMEM(counts.shape, jnp.int32),
+            pltpu.SMEM((blocks, span), jnp.float32),
             pltpu.SemaphoreType.DMA((3,)),
+            pltpu.SemaphoreType.DMA((3, cycle)),
             pltpu.SemaphoreType.DMA((3,)),
-            pltpu.SemaphoreType.DMA((3,)),
+            pltpu.SemaphoreType.DMA((2,)),
             pltpu.SemaphoreType.DMA,
             pltpu.SemaphoreType.DMA,
             pltpu.SemaphoreType.DMA,
@@ -267,7 +316,7 @@
             bytes_accessed=8 * rows * width,
             transcendentals=tokens * span * BLOCK,
         ),
-    )(queries, keys, values, bias)
+    )(queries, keys, values, key_blocks, counts)
 
 
 def solution(mesh):
@@ -282,7 +331,9 @@
     one_head_each = cycle * group * HD
 
     def chosen(queries, *others):
-        if queries.shape[1] == one_head_each and cycle >= 3:
+        rows = queries.shape[0]
+        aligned = QTILE % rows == 0 and rows * group % BLOCK == 0
+        if queries.shape[1] == one_head_each and cycle >= 3 and aligned:
             return local_heads(cycle, group, queries, *others)
         return local(queries, *others)
 

time: 114 us -> 101 us (0.89)
  Pallas kernels: 109 us -> 98.7 us
    pallas_call x1, Pallas kernels: 109 us -> 98.7 us  [local_heads(): pl.pallas_call(functools.partial(head_kernel, cycle, group, blocks_here),...]
    unnamed x5 -> x1, local copies, waits for them, and re-layouts: 2.94 us -> 2.29 us
where the time goes in v2:
time: 101 us
  Pallas kernels  98.7 us (98%)
  local copies, waits for them, and re-layouts  2.29 us (2%)
    pallas_call x1, Pallas kernels, local_heads(): pl.pallas_call(functools.partial(head_kernel, cycle, group, blocks_here),...  98.7 us
    unnamed x1, local copies, waits for them, and re-layouts  2.29 us

profile of v2, /device:TPU:1, one launch (start us, length us, event | category | flops | bytes accessed | tf_op | source)
XLA Modules:
  0.0 101.0 jit_solution(18360354574338601942)
XLA Ops:
  0.0 98.7 %shard_map.55 = bf16[128,4096]{1,0:T(8,128)(2,1)} custom-call(bf16[128,4096]{1,0:T(8,128)(2,1)} %q_ref.1, bf16[128,4096]{1,0:T(8,128)(2,1)} %k_ref.1, bf16[128,4096]{1,0:T(8,128)(2,1)} %v_ref.1, s32[8,6]{1,0:T(8,128)} %lists_ref.1, s32[8]{0:T(128)} %counts_ref.1), custom_call_target="tpu_custom_call" | custom-call | flops 6442450944 | bytes 4194304 | tf_op jit(solution)/shard_map/pallas_call | solution.py:290
  98.8 2.3 %copy.7 = bf16[128,4096]{1,0:T(8,128)(2,1)} copy(bf16[128,4096]{1,0:T(8,128)(2,1)} %shard_map.55) | data formatting | bytes 2097152

commit v3 on v2

--- a/solution.py
+++ b/solution.py
@@ -87,9 +87,15 @@
     inputs = ((k_ref, k_all), (q_ref, q_all), (v_ref, v_all))
 
     def target(step):
+        place = lax.rem(step, group)
+        ahead = lax.div(place, 2) + (1 - lax.rem(place, 2)) * (group // 2)
         blk = lax.rem(my_blk + lax.div(step, group), cycle)
-        head = lax.rem(my_head + lax.rem(step, group), group)
+        head = lax.rem(my_head + ahead, group)
         return blk, head
+
+    def each_partner(body):
+        body(0, 0)
+        lax.fori_loop(2, count, body, 0)
 
     def columns(device):
         return pl.ds(pl.multiple_of(device * HD, HD), HD)
@@ -103,7 +109,7 @@
         pl.semaphore_signal(barrier, inc=1, device_id=target(step), device_id_type=MESH)
         return carry
 
-    lax.fori_loop(1, count, greet, 0)
+    each_partner(greet)
     pl.semaphore_wait(barrier, count - 1)
 
     def send_all(index):
@@ -121,7 +127,7 @@
             ).start()
             return carry
 
-        lax.fori_loop(1, count, send, 0)
+        each_partner(send)
 
     def own_copy(index):
         source, gathered = inputs[index]
@@ -333,7 +339,7 @@
     def chosen(queries, *others):
         rows = queries.shape[0]
         aligned = QTILE % rows == 0 and rows * group % BLOCK == 0
-        if queries.shape[1] == one_head_each and cycle >= 3 and aligned:
+        if queries.shape[1] == one_head_each and cycle >= 3 and group % 2 == 0 and aligned:
             return local_heads(cycle, group, queries, *others)
         return local(queries, *others)
 

time: 101 us -> 99.9 us (0.989)
  Pallas kernels: 98.7 us -> 97.4 us
    pallas_call x1, Pallas kernels: 98.7 us -> 97.4 us  [local_heads(): pl.pallas_call(functools.partial(head_kernel, cycle, group, blocks_here),...]
where the time goes in v3:
time: 99.9 us; the launch traced here: 99.7 us
  Pallas kernels  97.4 us (97%)
  local copies, waits for them, and re-layouts  2.29 us (2%)
    pallas_call x1, Pallas kernels, local_heads(): pl.pallas_call(functools.partial(head_kernel, cycle, group, blocks_here),...  97.4 us
    unnamed x1, local copies, waits for them, and re-layouts  2.29 us

profile of v3, /device:TPU:1, one launch (start us, length us, event | category | flops | bytes accessed | tf_op | source)
XLA Modules:
  0.0 99.7 jit_solution(2869390346238441728)
XLA Ops:
  0.0 97.4 %shard_map.55 = bf16[128,4096]{1,0:T(8,128)(2,1)} custom-call(bf16[128,4096]{1,0:T(8,128)(2,1)} %q_ref.1, bf16[128,4096]{1,0:T(8,128)(2,1)} %k_ref.1, bf16[128,4096]{1,0:T(8,128)(2,1)} %v_ref.1, s32[8,6]{1,0:T(8,128)} %lists_ref.1, s32[8]{0:T(128)} %counts_ref.1), custom_call_target="tpu_custom_call" | custom-call | flops 6442450944 | bytes 4194304 | tf_op jit(solution)/shard_map/pallas_call | solution.py:296
  97.4 2.3 %copy.7 = bf16[128,4096]{1,0:T(8,128)(2,1)} copy(bf16[128,4096]{1,0:T(8,128)(2,1)} %shard_map.55) | data formatting | bytes 2097152

commit v4 on v3

--- a/solution.py
+++ b/solution.py
@@ -93,10 +93,6 @@
         head = lax.rem(my_head + ahead, group)
         return blk, head
 
-    def each_partner(body):
-        body(0, 0)
-        lax.fori_loop(2, count, body, 0)
-
     def columns(device):
         return pl.ds(pl.multiple_of(device * HD, HD), HD)
 
@@ -105,14 +101,12 @@
 
     barrier = pltpu.get_barrier_semaphore()
 
-    def greet(step, carry):
-        pl.semaphore_signal(barrier, inc=1, device_id=target(step), device_id_type=MESH)
-        return carry
-
-    each_partner(greet)
+    for step in range(count):
+        if step != 1:
+            pl.semaphore_signal(barrier, inc=1, device_id=target(step), device_id_type=MESH)
     pl.semaphore_wait(barrier, count - 1)
 
-    def send_all(index):
+    def send_group(index, back):
         source, gathered = inputs[index]
 
         def send(step, carry):
@@ -121,13 +115,17 @@
                 src_ref=source.at[:, columns(blk * group + head)],
                 dst_ref=gathered.at[rows_of(me), :],
                 send_sem=send_sem.at[index],
-                recv_sem=recv_sem.at[index, lax.div(step, group)],
+                recv_sem=recv_sem.at[index, back],
                 device_id=(blk, head),
                 device_id_type=MESH,
             ).start()
             return carry
 
-        each_partner(send)
+        if back == 0:
+            send(0, 0)
+            lax.fori_loop(2, group, send, 0)
+        else:
+            lax.fori_loop(back * group, (back + 1) * group, send, 0)
 
     def own_copy(index):
         source, gathered = inputs[index]
@@ -150,8 +148,14 @@
     def key_rows(block, j):
         return pl.ds(pl.multiple_of(key_block(block, j) * BLOCK, BLOCK), BLOCK)
 
-    send_all(0)
-    send_all(1)
+    later = (0,) + tuple(range(2, cycle))
+    for back in range(3):
+        send_group(0, back)
+    send_group(1, 1)
+    for back in range(3, cycle):
+        send_group(0, back)
+    for back in later:
+        send_group(1, back)
     for index in range(3):
         own_copy(index).start()
     list_copies = (
@@ -175,9 +179,10 @@
 
     lax.fori_loop(0, blocks, mark, 0)
 
+    for back in range(3):
+        arrived(0, back)
     for back in range(cycle):
-        arrived(0, back)
-    send_all(2)
+        send_group(2, back)
     tiles = BLOCK // QTILE
 
     def weigh(step, carry):
@@ -204,7 +209,7 @@
         return carry
 
     per_shard = blocks_here * tiles
-    for back in range(cycle):
+    def weigh_shard(back):
         arrived(1, back)
         first = lax.rem(my_blk + cycle - back, cycle) * per_shard
 
@@ -212,6 +217,12 @@
             return weigh(first + step, carry)
 
         lax.fori_loop(0, per_shard, weigh_here, 0)
+
+    weigh_shard(1)
+    for back in range(3, cycle):
+        arrived(0, back)
+    for back in later:
+        weigh_shard(back)
 
     owners = QTILE // rows
     my_place = lax.rem(lax.div(me * rows, BLOCK), blocks_here)

time: 99.9 us -> 99.6 us (level)
  no operation moved by 1% of the time
where the time goes in v4:
time: 99.6 us; the launch traced here: 99.4 us
  Pallas kernels  97.1 us (97%)
  local copies, waits for them, and re-layouts  2.29 us (2%)
    pallas_call x1, Pallas kernels, local_heads(): pl.pallas_call(functools.partial(head_kernel, cycle, group, blocks_here),...  97.1 us
    unnamed x1, local copies, waits for them, and re-layouts  2.29 us

profile of v4, /device:TPU:1, one launch (start us, length us, event | category | flops | bytes accessed | tf_op | source)
XLA Modules:
  0.0 99.4 jit_solution(11937058660965277192)
XLA Ops:
  0.0 97.1 %shard_map.55 = bf16[128,4096]{1,0:T(8,128)(2,1)} custom-call(bf16[128,4096]{1,0:T(8,128)(2,1)} %q_ref.1, bf16[128,4096]{1,0:T(8,128)(2,1)} %k_ref.1, bf16[128,4096]{1,0:T(8,128)(2,1)} %v_ref.1, s32[8,6]{1,0:T(8,128)} %lists_ref.1, s32[8]{0:T(128)} %counts_ref.1), custom_call_target="tpu_custom_call" | custom-call | flops 6442450944 | bytes 4194304 | tf_op jit(solution)/shard_map/pallas_call | solution.py:307
  97.1 2.3 %copy.7 = bf16[128,4096]{1,0:T(8,128)(2,1)} copy(bf16[128,4096]{1,0:T(8,128)(2,1)} %shard_map.55) | data formatting | bytes 2097152

commit v5 on v4

--- a/solution.py
+++ b/solution.py
@@ -227,10 +227,10 @@
     owners = QTILE // rows
     my_place = lax.rem(lax.div(me * rows, BLOCK), blocks_here)
 
-    def finish(shard, turn):
-        block = shard * blocks_here + lax.rem(my_place + 1 + turn, blocks_here)
-
-        def mix(tile, inner):
+    def finish(shard):
+        def mix(step, inner):
+            turn, tile = lax.rem(step, blocks_here), lax.div(step, blocks_here)
+            block = shard * blocks_here + lax.rem(my_place + 1 + turn, blocks_here)
             start = block * BLOCK + tile * QTILE
             here = pl.ds(pl.multiple_of(start, QTILE), QTILE)
             mixed = None
@@ -266,25 +266,21 @@
 
             return lax.fori_loop(0, owners, give, inner)
 
-        lax.fori_loop(0, tiles, mix, 0)
+        lax.fori_loop(0, blocks_here * tiles, mix, 0)
 
     for back in range(3):
         arrived(2, back)
 
-    def finish_previous(turn, carry):
-        finish(lax.rem(my_blk + cycle - 1, cycle), turn)
-        return carry
-
-    lax.fori_loop(0, blocks_here, finish_previous, 0)
+    finish(lax.rem(my_blk + cycle - 1, cycle))
     for back in range(3, cycle):
         arrived(2, back)
 
     def finish_rest(step, carry):
-        ahead = lax.rem(lax.rem(step, cycle - 1) + 1, cycle - 1)
-        finish(lax.rem(my_blk + ahead, cycle), lax.div(step, cycle - 1))
+        ahead = lax.rem(step + 1, cycle - 1)
+        finish(lax.rem(my_blk + ahead, cycle))
         return carry
 
-    lax.fori_loop(0, blocks_here * (cycle - 1), finish_rest, 0)
+    lax.fori_loop(0, cycle - 1, finish_rest, 0)
 
     pltpu.make_async_copy(
         o_all.at[rows_of(me), :], out_ref.at[:, columns(me)], out_own_sem
@@ -296,6 +292,30 @@
     pltpu.make_async_copy(others, others, out_recv_sem).wait()
 
 
+def rows_kernel(pieces, source, result, sems):
+    rows = source.shape[0] // pieces
+    copies = []
+    for piece in range(pieces):
+        here = pl.ds(piece * rows, rows)
+        copies.append(pltpu.make_async_copy(source.at[here], result.at[here], sems.at[piece]))
+    for copy in copies:
+        copy.start()
+    for copy in copies:
+        copy.wait()
+
+
+def place_rows(array):
+    pieces = array.shape[0] // 16
+    return pl.pallas_call(
+        functools.partial(rows_kernel, pieces),
+        out_shape=jax.ShapeDtypeStruct(array.shape, array.dtype),
+        in_specs=[pl.BlockSpec(memory_space=pl.ANY)],
+        out_specs=pl.BlockSpec(memory_space=pl.ANY),
+        scratch_shapes=[pltpu.SemaphoreType.DMA((pieces,))],
+        compiler_params=pltpu.CompilerParams(vmem_limit_bytes=60 * 2**20),
+    )(array)
+
+
 def local_heads(cycle, group, queries, keys, values, key_blocks, counts):
     rows, width = queries.shape
     tokens = rows * cycle * group
@@ -304,7 +324,7 @@
     span = 3 * blocks_here
     span = 3 * blocks_here
     whole = pltpu.VMEM((tokens, HD), jnp.bfloat16)
-    return pl.pallas_call(
+    attended = pl.pallas_call(
         functools.partial(head_kernel, cycle, group, blocks_here),
         out_shape=jax.ShapeDtypeStruct((rows, width), jnp.bfloat16),
         in_specs=[pl.BlockSpec(memory_space=pl.ANY)] * 5,
@@ -334,6 +354,7 @@
             transcendentals=tokens * span * BLOCK,
         ),
     )(queries, keys, values, key_blocks, counts)
+    return place_rows(attended)
 
 
 def solution(mesh):
@@ -349,7 +370,7 @@
 
     def chosen(queries, *others):
         rows = queries.shape[0]
-        aligned = QTILE % rows == 0 and rows * group % BLOCK == 0
+        aligned = QTILE % rows == 0 and rows % 16 == 0 and rows * group % BLOCK == 0
         if queries.shape[1] == one_head_each and cycle >= 3 and group % 2 == 0 and aligned:
             return local_heads(cycle, group, queries, *others)
         return local(queries, *others)

time: 99.6 us -> 130 us (1.31)
  Pallas kernels: 97.1 us -> 130 us
  local copies, waits for them, and re-layouts: 2.29 us -> 0 us
    pallas_call x0 -> x1, Pallas kernels: none -> 32.9 us  [place_rows(): pl.pallas_call(functools.partial(rows_kernel, pieces), out_shape=jax.Shap...]
    unnamed x1 -> x0, local copies, waits for them, and re-layouts: 2.29 us -> none
where the time goes in v5:
time: 130 us
  Pallas kernels  130 us (100%)
    pallas_call x1, Pallas kernels, local_heads(): pl.pallas_call(functools.partial(head_kernel, cycle, group, blocks_here),...  97.2 us
    pallas_call x1, Pallas kernels, place_rows(): pl.pallas_call(functools.partial(rows_kernel, pieces), out_shape=jax.Shap...  32.9 us

profile of v5, /device:TPU:1, one launch (start us, length us, event | category | flops | bytes accessed | tf_op | source)
XLA Modules:
  0.0 130.1 jit_solution(9828221663356803065)
XLA Ops:
  0.0 97.2 %shard_map.55.source = bf16[128,4096]{1,0:T(8,128)(2,1)} custom-call(bf16[128,4096]{1,0:T(8,128)(2,1)} %q_ref.1, bf16[128,4096]{1,0:T(8,128)(2,1)} %k_ref.1, bf16[128,4096]{1,0:T(8,128)(2,1)} %v_ref.1, s32[8,6]{1,0:T(8,128)} %lists_ref.1, s32[8]{0:T(128)} %counts_ref.1), custom_call_target="tpu_custom_call" | custom-call | flops 6442450944 | bytes 4194304 | tf_op jit(solution)/shard_map/pallas_call | solution.py:327
  97.2 32.9 %shard_map.56 = bf16[128,4096]{1,0:T(8,128)(2,1)} custom-call(bf16[128,4096]{1,0:T(8,128)(2,1)} %shard_map.55.source), custom_call_target="tpu_custom_call" | custom-call | tf_op jit(solution)/shard_map/pallas_call | solution.py:309

commit v6 on v5

--- a/solution.py
+++ b/solution.py
@@ -292,26 +292,19 @@
     pltpu.make_async_copy(others, others, out_recv_sem).wait()
 
 
-def rows_kernel(pieces, source, result, sems):
-    rows = source.shape[0] // pieces
-    copies = []
-    for piece in range(pieces):
-        here = pl.ds(piece * rows, rows)
-        copies.append(pltpu.make_async_copy(source.at[here], result.at[here], sems.at[piece]))
-    for copy in copies:
-        copy.start()
-    for copy in copies:
-        copy.wait()
+def rows_kernel(source, result):
+    result[...] = source[...]
 
 
 def place_rows(array):
-    pieces = array.shape[0] // 16
+    rows, width = array.shape
+    piece = pl.BlockSpec((rows // 4, width), lambda step: (step, 0))
     return pl.pallas_call(
-        functools.partial(rows_kernel, pieces),
+        rows_kernel,
+        grid=(4,),
         out_shape=jax.ShapeDtypeStruct(array.shape, array.dtype),
-        in_specs=[pl.BlockSpec(memory_space=pl.ANY)],
-        out_specs=pl.BlockSpec(memory_space=pl.ANY),
-        scratch_shapes=[pltpu.SemaphoreType.DMA((pieces,))],
+        in_specs=[piece],
+        out_specs=piece,
         compiler_params=pltpu.CompilerParams(vmem_limit_bytes=60 * 2**20),
     )(array)
 
@@ -370,7 +363,7 @@
 
     def chosen(queries, *others):
         rows = queries.shape[0]
-        aligned = QTILE % rows == 0 and rows % 16 == 0 and rows * group % BLOCK == 0
+        aligned = QTILE % rows == 0 and rows % 64 == 0 and rows * group % BLOCK == 0
         if queries.shape[1] == one_head_each and cycle >= 3 and group % 2 == 0 and aligned:
             return local_heads(cycle, group, queries, *others)
         return local(queries, *others)

time: 130 us -> 101 us (0.78)
  Pallas kernels: 130 us -> 101 us
    pallas_call x1, Pallas kernels: 32.9 us -> 3.37 us  [place_rows(): pl.pallas_call(rows_kernel, grid=(4,), out_shape=jax.ShapeDtypeStruct(arr...]
where the time goes in v6:
time: 101 us
  Pallas kernels  101 us (100%)
    pallas_call x1, Pallas kernels, local_heads(): pl.pallas_call(functools.partial(head_kernel, cycle, group, blocks_here),...  97.2 us
    pallas_call x1, Pallas kernels, place_rows(): pl.pallas_call(rows_kernel, grid=(4,), out_shape=jax.ShapeDtypeStruct(arr...  3.37 us

profile of v6, /device:TPU:1, one launch (start us, length us, event | category | flops | bytes accessed | tf_op | source)
XLA Modules:
  0.0 100.5 jit_solution(14976322996070461840)
XLA Ops:
  0.0 97.2 %shard_map.55.source = bf16[128,4096]{1,0:T(8,128)(2,1)} custom-call(bf16[128,4096]{1,0:T(8,128)(2,1)} %q_ref.1, bf16[128,4096]{1,0:T(8,128)(2,1)} %k_ref.1, bf16[128,4096]{1,0:T(8,128)(2,1)} %v_ref.1, s32[8,6]{1,0:T(8,128)} %lists_ref.1, s32[8]{0:T(128)} %counts_ref.1), custom_call_target="tpu_custom_call" | custom-call | flops 6442450944 | bytes 4194304 | tf_op jit(solution)/shard_map/pallas_call | solution.py:320
  97.2 3.4 %shard_map.56 = bf16[128,4096]{1,0:T(8,128)(2,1)} custom-call(bf16[128,4096]{1,0:T(8,128)(2,1)} %shard_map.55.source), custom_call_target="tpu_custom_call" | custom-call | tf_op jit(solution)/shard_map/pallas_call | solution.py:302

commit v7 on v4

--- a/solution.py
+++ b/solution.py
@@ -123,9 +123,9 @@
 
         if back == 0:
             send(0, 0)
-            lax.fori_loop(2, group, send, 0)
+            lax.fori_loop(2, group, send, 0, unroll=True)
         else:
-            lax.fori_loop(back * group, (back + 1) * group, send, 0)
+            lax.fori_loop(back * group, (back + 1) * group, send, 0, unroll=True)
 
     def own_copy(index):
         source, gathered = inputs[index]

time: 99.6 us -> 99.6 us (level)
  no operation moved by 1% of the time
where the time goes in v7:
time: 99.6 us; the launch traced here: 99.4 us
  Pallas kernels  97.1 us (97%)
  local copies, waits for them, and re-layouts  2.29 us (2%)
    pallas_call x1, Pallas kernels, local_heads(): pl.pallas_call(functools.partial(head_kernel, cycle, group, blocks_here),...  97.1 us
    unnamed x1, local copies, waits for them, and re-layouts  2.29 us

profile of v7, /device:TPU:1, one launch (start us, length us, event | category | flops | bytes accessed | tf_op | source)
XLA Modules:
  0.0 99.4 jit_solution(15909110778823151170)
XLA Ops:
  0.0 97.1 %shard_map.55 = bf16[128,4096]{1,0:T(8,128)(2,1)} custom-call(bf16[128,4096]{1,0:T(8,128)(2,1)} %q_ref.1, bf16[128,4096]{1,0:T(8,128)(2,1)} %k_ref.1, bf16[128,4096]{1,0:T(8,128)(2,1)} %v_ref.1, s32[8,6]{1,0:T(8,128)} %lists_ref.1, s32[8]{0:T(128)} %counts_ref.1), custom_call_target="tpu_custom_call" | custom-call | flops 6442450944 | bytes 4194304 | tf_op jit(solution)/shard_map/pallas_call | solution.py:307
  97.1 2.3 %copy.7 = bf16[128,4096]{1,0:T(8,128)(2,1)} copy(bf16[128,4096]{1,0:T(8,128)(2,1)} %shard_map.55) | data formatting | bytes 2097152
